TPU v7x, 32 devices: a whole 2x2x4 slice. The times are simulated.
32 devices in a mesh: ep: 16 (over z, y, core), dp: 2 (over x).
Axes of the slice: x: 2, y: 2, z: 4, core: 2. Of those that a mesh axis runs over, the one named last changes fastest.
Arguments:
- out_grad: bfloat16 [4096, 3584], P(('ep', 'dp')), may hold values from -6 to 6
- expert_ids: int32 [4096, 2], P(('ep', 'dp')), may hold values from 0 to 15, all different within a row; in each aligned block of 128 rows (0 to 127, 128 to 255, ...) at most 24 rows name the same one
- combine: float32 [4096, 2], P(('ep', 'dp')), may hold values from 0.1 to 1
- router_logits: bfloat16 [4096, 384], P(('ep', 'dp')), may hold values from -16 to 250
- saved_hidden: bfloat16 [16, 768, 1024], P('ep', 'dp'), may hold values from -6 to 6
- weight: bfloat16 [16, 1024, 3584], P('ep', 'dp'), may hold values from -0.1875 to 0.1875
- moment_one: bfloat16 [16, 1024, 3584], P('ep', 'dp'), may hold values from -6 to 6
- moment_two: bfloat16 [16, 1024, 3584], P('ep', 'dp'), may hold values from 2 to 40
- next_hidden: bfloat16 [16, 64, 1024], P('ep', 'dp'), may hold values from -6 to 6
Outputs:
- refreshed: bfloat16 [16, 64, 3584], P('ep', 'dp')
- router_grad: bfloat16 [4096, 384], P(('ep', 'dp'))
Inputs may be any that keep to these rules, and one draw needn't show every extreme that they name: `expert_ids`: each row names 2 different experts; among the 128 rows of one device no expert is named more than 24 times, a bound that some block reaches.
All inputs are finite; a program needn't handle non-finite values.
Results may differ from a plain program's by a relative error of at most 0.014.
Values may be sent and summed in bfloat16 or wider, within the bound.
A program may use at most 64 MiB of HBM per device.

v0:
```python
import jax
import jax.numpy as jnp
from jax import lax
from jax.sharding import PartitionSpec as P

beta_one = 0.9
beta_two = 0.95
learn_rate = 0.2
decay_rate = 0.1
step_count = 100.0
adam_eps = 1e-08
zloss_coef = 0.25


def adamw(weight, first, second, gradient):
    first_new = beta_one * first.astype(jnp.float32) + (1.0 - beta_one) * gradient
    second_new = beta_two * second.astype(jnp.float32) + (1.0 - beta_two) * gradient * gradient
    first_hat = first_new / (1.0 - beta_one**step_count)
    second_hat = second_new / (1.0 - beta_two**step_count)
    current = weight.astype(jnp.float32)
    change = first_hat / (jnp.sqrt(second_hat) + adam_eps) + decay_rate * current
    return (current - learn_rate * change).astype(jnp.bfloat16)


def zloss_grad(logits):
    values = logits.astype(jnp.float32)
    row_max = jnp.max(values, axis=-1, keepdims=True)
    log_total = row_max + jnp.log(jnp.sum(jnp.exp(values - row_max), axis=-1, keepdims=True))
    probs = jnp.exp(values - log_total)
    return (zloss_coef * 2.0 * log_total * probs).astype(jnp.bfloat16)


def per_device(
    out_grad,
    expert_ids,
    combine,
    router_logits,
    saved_hidden,
    weight,
    moment_one,
    moment_two,
    next_hidden,
):
    experts_count = lax.axis_size("ep")
    replicas = lax.axis_size("dp")
    rows_total = saved_hidden.shape[1]
    capacity = rows_total // experts_count
    model_width = out_grad.shape[1]
    slab_rows = weight.shape[1]
    flat_ids = expert_ids.reshape(-1)
    onehot = (flat_ids[:, None] == jnp.arange(experts_count, dtype=jnp.int32)[None, :]).astype(
        jnp.int32
    )
    before = jnp.cumsum(onehot, axis=0) - onehot
    slot_index = jnp.sum(before * onehot, axis=1)
    target = flat_ids * capacity + slot_index
    scaled = (combine[:, :, None] * out_grad[:, None, :].astype(jnp.float32)).astype(jnp.bfloat16)
    scaled = scaled.reshape(-1, model_width)
    send_rows = jnp.zeros((rows_total, model_width), jnp.bfloat16).at[target].set(scaled)
    received = lax.all_to_all(
        send_rows.reshape(experts_count, capacity, model_width),
        "ep",
        split_axis=0,
        concat_axis=0,
        tiled=True,
    )
    received = received.reshape(rows_total, model_width)
    router_grad = zloss_grad(router_logits)
    partial_value = lax.dot_general(
        saved_hidden[0], received, (((0,), (0,)), ((), ())), preferred_element_type=jnp.float32
    )
    slabs = partial_value.astype(jnp.bfloat16).reshape(replicas, slab_rows, model_width)
    collected = lax.all_to_all(slabs, "dp", split_axis=0, concat_axis=0, tiled=True)
    gradient = jnp.sum(collected.astype(jnp.float32), axis=0)
    updated = adamw(weight[0], moment_one[0], moment_two[0], gradient)
    hidden_rows = next_hidden[0]
    refreshed = jnp.dot(
        hidden_rows,
        lax.all_gather(updated, "dp", axis=0, tiled=True),
        preferred_element_type=jnp.float32,
    )
    return (refreshed.astype(jnp.bfloat16)[None], router_grad)


def solution(mesh):
    in_specs = (
        P(("ep", "dp"), None),
        P(("ep", "dp"), None),
        P(("ep", "dp"), None),
        P(("ep", "dp"), None),
        P("ep", "dp", None),
        P("ep", "dp", None),
        P("ep", "dp", None),
        P("ep", "dp", None),
        P("ep", "dp", None),
    )
    out_specs = (P("ep", "dp", None), P(("ep", "dp"), None))
    return jax.shard_map(
        per_device, mesh=mesh, in_specs=in_specs, out_specs=out_specs, check_vma=False
    )
```

profile of v0, /device:TPU:0, one launch (start us, length us, event | category | flops | bytes accessed | tf_op | source)
XLA Modules:
  0.0 302.2 jit_solution(13486980231349769000)
XLA Ops:
  7.2 0.0 copy-start
  7.2 0.0 copy-start.4
  7.2 0.0 all-gather.2.cloned.1.call-start
  7.2 0.7 broadcast_multiply_fusion
  8.0 0.8 copy.12
  8.8 0.1 eq.25
  8.9 0.1 eq.29
  9.0 0.1 copy.11
  9.2 0.1 mul.100
  9.3 0.6 reduce-window.6
  9.9 0.2 slice_reduce_fusion
  10.1 3.9 %mul.104 = f32[128,2,3584]{2,1,0:T(2,128)} broadcast(bf16[128,3584]{1,0:T(8,128)(2,1)} %param.9), dimensions={0,2} | broadcast | bytes 4587520 | tf_op jit(solution)/shard_map/mul | solution.py:57
  14.1 5.7 %mul.105 = f32[256,3584]{1,0:T(8,128)} reshape(f32[128,2,3584]{2,1,0:T(2,128)} %mul.104) | data formatting | bytes 7340032 | tf_op jit(solution)/shard_map/mul | solution.py:57
  19.7 0.0 copy-done.4
  19.7 0.1 copy.15
  19.9 0.1 mul.102
  20.0 0.1 fusion.22
  20.1 5.5 %scatter_custom_fusion = bf16[384,3584]{1,0:T(8,128)(2,1)S(1)} fusion(s32[256]{0:T(256)S(1)} %bitcast.53, f32[256,3584]{1,0:T(8,128)} %mul.105, f32[256]{0:T(256)S(1)} %mul.102, bf16[]{:T(256)} %constant.16.clone.1), kind=kCustom, calls=%fused_computation.19 | custom fusion | flops 1835008 | bytes 6423554 | tf_op jit(solution)/shard_map/scatter | solution.py:59
  25.6 70.4 %all_to_all.10 = bf16[16,24,3584]{2,1,0:T(8,128)(2,1)S(1)} all-to-all(bf16[16,24,3584]{2,1,0:T(8,128)(2,1)S(1)} %bitcast.49), channel_id=1, replica_groups=mesh['ep'=16,'dp'=2] {'ep'}, dimensions={0} | all-to-all | bytes 5505024 | tf_op jit(solution)/shard_map/all_to_all | solution.py:60
  96.0 0.0 copy-done
  96.0 4.3 %convolution_convert_fusion = bf16[3584,1024]{0,1:T(8,128)(2,1)S(1)} fusion(bf16[384,3584]{1,0:T(8,128)(2,1)S(1)} %bitcast.51, bf16[1,384,1024]{2,1,0:T(8,128)(2,1)S(1)} %copy-done), kind=kOutput, calls=%fused_computation.5 | convolution fusion | flops 2822242304 | bytes 10878976 | tf_op jit(solution)/shard_map/dot_general | solution.py:69
  100.3 84.8 %all_to_all.11 = bf16[2,512,3584]{2,1,0:T(8,128)(2,1)S(1)} all-to-all(bf16[2,512,3584]{2,1,0:T(8,128)(2,1)S(1)} %bitcast.50), channel_id=1, replica_groups=mesh['ep'=16,'dp'=2] {'dp'}, dimensions={0} | all-to-all | bytes 14680064 | tf_op jit(solution)/shard_map/all_to_all | solution.py:73
  185.1 0.0 copy-start.1
  185.1 4.2 %convert_reduce_fusion = f32[512,3584]{1,0:T(8,128)} fusion(bf16[2,512,3584]{2,1,0:T(8,128)(2,1)S(1)} %all_to_all.11), kind=kLoop, calls=%fused_computation.1 | loop fusion | flops 5505024 | bytes 14680064 | tf_op jit(solution)/shard_map/reduce_sum | solution.py:74
  189.3 0.0 copy-done.1
  189.3 0.0 copy-start.2
  189.3 0.0 copy-start.3
  189.3 10.9 %fusion.2 = bf16[512,3584]{1,0:T(8,128)(2,1)} fusion(f32[512,3584]{1,0:T(8,128)} %convert_reduce_fusion, bf16[1,512,3584]{2,1,0:T(8,128)(2,1)S(1)} %copy-done.1, bf16[1,512,3584]{2,1,0:T(8,128)(2,1)} %param.15, bf16[1,512,3584]{2,1,0:T(8,128)(2,1)} %param.14), kind=kLoop, calls=%fused_computation.8 | loop fusion | flops 34865152 | bytes 22020096 | tf_op jit(solution)/shard_map/convert_element_type | solution.py:22
  200.2 0.0 all-gather.2.cloned.1.call-update
  200.2 0.0 copy-done.2
  200.2 0.1 reduce_max.14
  200.3 0.2 fusion.15
  200.5 0.8 fusion.18
  201.3 88.9 %all-gather.2.cloned.1.call-done = bf16[1024,3584]{1,0:T(8,128)(2,1)} async-done(((bf16[512,3584]{1,0:T(8,128)(2,1)}), bf16[1024,3584]{1,0:T(8,128)(2,1)}) %all-gather.2.cloned.1.call-update) | async-done | bytes 7340048 | tf_op jit(solution)/shard_map/all_gather | solution.py:79
  290.2 0.0 copy-done.3
  290.2 5.1 %fusion.9 = bf16[1,32,3584]{2,1,0:T(8,128)(2,1)} fusion(bf16[1024,3584]{1,0:T(8,128)(2,1)} %all-gather.2.cloned.1.call-done, bf16[1,32,1024]{2,1,0:T(8,128)(2,1)S(1)} %copy-done.3), kind=kOutput, calls=%fused_computation.17 | convolution fusion | flops 234995712 | bytes 7634944 | tf_op jit(solution)/shard_map/dot_general | solution.py:77
  (6 shorter events, 0.1 us)
Async XLA Ops:
  7.2 88.9 %copy-start = (bf16[1,384,1024]{2,1,0:T(8,128)(2,1)S(1)}, bf16[1,384,1024]{2,1,0:T(8,128)(2,1)}, u32[]{:S(2)}) copy-start(bf16[1,384,1024]{2,1,0:T(8,128)(2,1)} %param.13) | copy-start | bytes 2359300
  7.2 12.6 %copy-start.4 = (f32[128,2]{0,1:T(2,128)S(1)}, f32[128,2]{0,1:T(2,128)}, u32[]{:S(2)}) copy-start(f32[128,2]{0,1:T(2,128)} %param.11) | copy-start | bytes 3076
  7.2 283.0 %all-gather.2.cloned.1.call-start = ((), (), s32[]{:S(2)}) async-start(), calls=%async_computation.2 | async-start | bytes 11010048 | tf_op jit(solution)/shard_map/all_gather | solution.py:79
  185.1 4.2 %copy-start.1 = (bf16[1,512,3584]{2,1,0:T(8,128)(2,1)S(1)}, bf16[1,512,3584]{2,1,0:T(8,128)(2,1)}, u32[]{:S(2)}) copy-start(bf16[1,512,3584]{2,1,0:T(8,128)(2,1)} %param.16) | copy-start | bytes 11010052
  189.3 10.9 %copy-start.2 = (bf16[128,384]{1,0:T(8,128)(2,1)S(1)}, bf16[128,384]{1,0:T(8,128)(2,1)}, u32[]{:S(2)}) copy-start(bf16[128,384]{1,0:T(8,128)(2,1)} %param.12) | copy-start | bytes 294916
  189.3 100.9 %copy-start.3 = (bf16[1,32,1024]{2,1,0:T(8,128)(2,1)S(1)}, bf16[1,32,1024]{2,1,0:T(8,128)(2,1)}, u32[]{:S(2)}) copy-start(bf16[1,32,1024]{2,1,0:T(8,128)(2,1)} %param.17) | copy-start | bytes 196612
Sparse Core Ops, SparseCore 0:
  200.3 89.8 all-gather.1
where the time goes:
time: 303 us; the launch traced here: 302 us
  blocking collectives  155 us (51%)
  waiting for transfers between devices  89 us (29%)
  other arithmetic  23.1 us (8%)
  between operations  14.1 us (5%)
  local copies, waits for them, and re-layouts  11.4 us (4%)
  matrix products  9.45 us (3%)
    all_gather x1, waiting for transfers between devices, per_device(): lax.all_gather(updated, 'dp', axis=0, tiled=True)  88.9 us
    all_to_all x1, blocking collectives, per_device(): lax.all_to_all(slabs, 'dp', split_axis=0, concat_axis=0, tiled=True)  84.8 us
    all_to_all x1, blocking collectives, per_device(): lax.all_to_all(send_rows.reshape(experts_count, capacity, model_width), '...  70.4 us
    convert_element_type x1, other arithmetic, adamw(): return (current - learn_rate * change).astype(jnp.bfloat16)  10.9 us
    mul x3, local copies, waits for them, and re-layouts, per_device(): combine[:, :, None] * out_grad[:, None, :].astype(jnp.float32)  9.74 us
  transfers between devices with their start and end apart: 1, of which 1 were waited for; matrix products, arithmetic and copies ran while one was open for 0% of the time, Pallas kernels for 0%

commit v1 on v0

--- a/solution.py
+++ b/solution.py
@@ -66,19 +66,37 @@
     )
     received = received.reshape(rows_total, model_width)
     router_grad = zloss_grad(router_logits)
-    partial_value = lax.dot_general(
-        saved_hidden[0], received, (((0,), (0,)), ((), ())), preferred_element_type=jnp.float32
-    )
-    slabs = partial_value.astype(jnp.bfloat16).reshape(replicas, slab_rows, model_width)
-    collected = lax.all_to_all(slabs, "dp", split_axis=0, concat_axis=0, tiled=True)
-    gradient = jnp.sum(collected.astype(jnp.float32), axis=0)
+    if replicas == 2:
+        hidden_parts = saved_hidden[0].reshape(rows_total, replicas, slab_rows).swapaxes(0, 1)
+        hidden_parts = lax.all_to_all(hidden_parts, "dp", split_axis=0, concat_axis=0, tiled=True)
+        me = lax.axis_index("dp")
+        other_rows = lax.ppermute(received, "dp", [(0, 1), (1, 0)])
+        own_hidden = lax.dynamic_index_in_dim(hidden_parts, me, 0, keepdims=False)
+        other_hidden = lax.dynamic_index_in_dim(hidden_parts, 1 - me, 0, keepdims=False)
+        gradient = lax.dot_general(
+            own_hidden, received, (((0,), (0,)), ((), ())), preferred_element_type=jnp.float32
+        ) + lax.dot_general(
+            other_hidden, other_rows, (((0,), (0,)), ((), ())), preferred_element_type=jnp.float32
+        )
+    else:
+        partial_value = lax.dot_general(
+            saved_hidden[0], received, (((0,), (0,)), ((), ())), preferred_element_type=jnp.float32
+        )
+        slabs = partial_value.astype(jnp.bfloat16).reshape(replicas, slab_rows, model_width)
+        collected = lax.all_to_all(slabs, "dp", split_axis=0, concat_axis=0, tiled=True)
+        gradient = jnp.sum(collected.astype(jnp.float32), axis=0)
     updated = adamw(weight[0], moment_one[0], moment_two[0], gradient)
-    hidden_rows = next_hidden[0]
-    refreshed = jnp.dot(
-        hidden_rows,
-        lax.all_gather(updated, "dp", axis=0, tiled=True),
+    next_rows = next_hidden.shape[1]
+    hidden_slabs = next_hidden[0].reshape(next_rows, replicas, slab_rows).swapaxes(0, 1)
+    hidden_slabs = lax.all_to_all(hidden_slabs, "dp", split_axis=0, concat_axis=0, tiled=True)
+    product = jnp.dot(
+        hidden_slabs.reshape(replicas * next_rows, slab_rows),
+        updated,
         preferred_element_type=jnp.float32,
     )
+    product = product.astype(jnp.bfloat16).reshape(replicas, next_rows, model_width)
+    product = lax.all_to_all(product, "dp", split_axis=0, concat_axis=0, tiled=True)
+    refreshed = jnp.sum(product.astype(jnp.float32), axis=0)
     return (refreshed.astype(jnp.bfloat16)[None], router_grad)
 
 

time: 303 us -> 197 us (0.65)
  blocking collectives: 155 us -> 70.7 us
  waiting for transfers between devices: 89 us -> 65.5 us
  between operations: 14.1 us -> 0.72 us
  starting transfers between devices: 0.04 us -> 12.6 us
  other arithmetic: 23.1 us -> 11.6 us
  matrix products: 9.45 us -> 19.5 us
  local copies, waits for them, and re-layouts: 11.4 us -> 15.5 us
    all_gather x1 -> x0, waiting for transfers between devices: 88.9 us -> none  [per_device(): lax.all_gather(updated, 'dp', axis=0, tiled=True)]
    all_to_all x1 -> x0, blocking collectives: 84.8 us -> none  [per_device(): lax.all_to_all(slabs, 'dp', split_axis=0, concat_axis=0, tiled=True)]
    all_to_all x0 -> x3, waiting for transfers between devices: none -> 65.5 us  [the longest x1 59.1 us: per_device(): lax.all_to_all(hidden_parts, 'dp', split_axis=0, concat_axis=0, tiled=True)]
    all_to_all x0 -> x3, starting transfers between devices: none -> 11.1 us  [the longest x1 4.08 us: per_device(): lax.all_to_all(hidden_slabs, 'dp', split_axis=0, concat_axis=0, tiled=True)]
    convert_element_type x1 -> x0, other arithmetic: 10.9 us -> none  [adamw(): return (current - learn_rate * change).astype(jnp.bfloat16)]
    dot_general x2, matrix products: 9.45 us -> 19.5 us  [the longest x1 14.4 us: per_device(): jnp.dot(hidden_slabs.reshape(replicas * next_rows, slab_rows), updated, p...]
    reduce_sum x1, other arithmetic: 4.16 us -> 0.8 us  [per_device(): refreshed = jnp.sum(product.astype(jnp.float32), axis=0)]
  transfers between devices with their start and end apart: 1 -> 4, of which waited for: 1 -> 2; matrix products, arithmetic and copies ran while one was open for 0% -> 6% of each run, Pallas kernels for 0% -> 0%
where the time goes in v1:
time: 197 us; the launch traced here: 196 us
  blocking collectives  70.7 us (36%)
  waiting for transfers between devices  65.5 us (33%)
  matrix products  19.5 us (10%)
  local copies, waits for them, and re-layouts  15.5 us (8%)
  starting transfers between devices  12.6 us (6%)
  other arithmetic  11.6 us (6%)
    all_to_all x1, blocking collectives, per_device(): lax.all_to_all(send_rows.reshape(experts_count, capacity, model_width), '...  70.7 us
    all_to_all x1, waiting for transfers between devices, per_device(): lax.all_to_all(hidden_parts, 'dp', split_axis=0, concat_axis=0, tiled=True)  59.1 us
    dot_general x1, matrix products, per_device(): jnp.dot(hidden_slabs.reshape(replicas * next_rows, slab_rows), updated, p...  14.4 us
    mul x3, local copies, waits for them, and re-layouts, per_device(): combine[:, :, None] * out_grad[:, None, :].astype(jnp.float32)  9.75 us
    scatter x1, other arithmetic, per_device(): jnp.zeros((rows_total, model_width), jnp.bfloat16).at[target].set(scaled)  6.54 us
    all_to_all x1, waiting for transfers between devices, per_device(): lax.all_to_all(product, 'dp', split_axis=0, concat_axis=0, tiled=True)  6.44 us
    dot_general x1, matrix products, per_device(): lax.dot_general(own_hidden, received, (((0,), (0,)), ((), ())), preferred...  5.04 us
    all_to_all x1, starting transfers between devices, per_device(): lax.all_to_all(hidden_slabs, 'dp', split_axis=0, concat_axis=0, tiled=True)  4.08 us
  transfers between devices with their start and end apart: 4, of which 2 were waited for; matrix products, arithmetic and copies ran while one was open for 6% of the time, Pallas kernels for 0%

profile of v1, /device:TPU:0, one launch (start us, length us, event | category | flops | bytes accessed | tf_op | source)
XLA Modules:
  0.0 196.0 jit_solution(8242564784528570880)
XLA Ops:
  0.6 0.8 copy.28
  1.4 0.1 eq.29
  1.6 0.1 eq.25
  1.7 0.7 broadcast_multiply_fusion
  2.4 0.6 reduce-window.6
  3.0 0.2 slice_reduce_fusion
  3.2 0.1 copy.27
  3.3 0.1 mul.100
  3.5 4.0 %mul.104 = f32[128,2,3584]{2,1,0:T(2,128)} broadcast(bf16[128,3584]{1,0:T(8,128)(2,1)} %param.9), dimensions={0,2} | broadcast | bytes 4587520 | tf_op jit(solution)/shard_map/mul | solution.py:57
  7.4 0.0 copy-start.2
  7.4 5.6 %mul.105 = f32[256,3584]{1,0:T(8,128)} reshape(f32[128,2,3584]{2,1,0:T(2,128)} %mul.104) | data formatting | bytes 7340032 | tf_op jit(solution)/shard_map/mul | solution.py:57
  13.1 0.0 copy-done.2
  13.1 0.1 copy.31
  13.2 0.1 mul.102
  13.3 0.1 fusion.26
  13.4 6.5 %scatter_custom_fusion = bf16[384,3584]{1,0:T(8,128)(2,1)} fusion(s32[256]{0:T(256)S(1)} %bitcast.67, f32[256,3584]{1,0:T(8,128)} %mul.105, f32[256]{0:T(256)S(1)} %mul.102, bf16[]{:T(256)} %constant.14.clone.1), kind=kCustom, calls=%fused_computation.16 | custom fusion | flops 1835008 | bytes 6423554 | tf_op jit(solution)/shard_map/scatter | solution.py:59
  20.0 0.0 copy-start.1
  20.0 70.7 %all_to_all.20 = bf16[16,24,3584]{2,1,0:T(8,128)(2,1)S(1)} all-to-all(bf16[16,24,3584]{2,1,0:T(8,128)(2,1)} %bitcast.63), channel_id=1, replica_groups=mesh['ep'=16,'dp'=2] {'ep'}, dimensions={0} | all-to-all | bytes 5505024 | tf_op jit(solution)/shard_map/all_to_all | solution.py:60
  90.7 1.5 collective-permute-start
  92.2 0.0 copy-done.1
  92.2 1.2 copy.25
  93.3 3.5 %all-to-all-start = ((bf16[2,384,512]{1,2,0:T(8,128)(2,1)}), bf16[2,384,512]{1,2,0:T(8,128)(2,1)S(1)}, u32[]{:S(2)}, u32[]{:S(2)}) async-start(bf16[2,384,512]{1,2,0:T(8,128)(2,1)} %bitcast.3), calls=%async_computation | async-start | bytes 1572864 | tf_op jit(solution)/shard_map/all_to_all | solution.py:71
  96.9 1.5 reshape_squeeze.7
  98.4 1.5 copy.33
  99.8 1.0 reduce_max.14
  100.9 1.1 fusion.20
  101.9 59.1 %all-to-all-done = bf16[2,384,512]{1,2,0:T(8,128)(2,1)S(1)} async-done(((bf16[2,384,512]{1,2,0:T(8,128)(2,1)}), bf16[2,384,512]{1,2,0:T(8,128)(2,1)S(1)}, u32[]{:S(2)}, u32[]{:S(2)}) %all-to-all-start) | async-done | bytes 786464 | tf_op jit(solution)/shard_map/all_to_all | solution.py:71
  161.0 4.1 %all-to-all-start.2 = ((bf16[2,32,512]{2,1,0:T(8,128)(2,1)}), bf16[2,32,512]{2,1,0:T(8,128)(2,1)}, u32[]{:S(2)}, u32[]{:S(2)}) async-start(bf16[2,32,512]{2,1,0:T(8,128)(2,1)} %copy.33), calls=%async_computation.2 | async-start | bytes 131072 | tf_op jit(solution)/shard_map/all_to_all | solution.py:91
  165.1 5.0 %fusion.14 = f32[512,3584]{1,0:T(8,128)} fusion(bf16[384,3584]{1,0:T(8,128)(2,1)S(1)} %bitcast.62, bf16[2,384,512]{1,2,0:T(8,128)(2,1)S(1)} %all-to-all-done, s32[]{:T(128)S(6)} %select_n.17), kind=kOutput, calls=%fused_computation.20 | convolution fusion | flops 1409286144 | bytes 10485764 | tf_op jit(solution)/shard_map/dot_general | solution.py:76
  170.1 0.0 all-to-all-done.2
  170.1 0.0 collective-permute-done
  170.1 0.0 copy-start
  170.1 14.4 %convolution_convert_fusion = bf16[3584,64]{0,1:T(8,128)(2,1)} fusion(bf16[64,512]{1,0:T(8,128)(2,1)} %bitcast.14, bf16[1,512,3584]{2,1,0:T(8,128)(2,1)} %param.16, f32[512,3584]{1,0:T(8,128)} %fusion.14, bf16[1,512,3584]{2,1,0:T(8,128)(2,1)} %param.15, bf16[384,3584]{1,0:T(8,128)(2,1)} %collective-permute-done, bf16[1,512,3584]{2,1,0:T(8,128)(2,1)} %param.14, ...), kind=kOutput, calls=%fused_computation.14 | convolution fusion | flops 1681096704 | bytes 22020100 | tf_op jit(solution)/shard_map/dot_general | solution.py:92
  184.5 3.5 %all-to-all-start.3 = ((bf16[2,32,3584]{2,1,0:T(8,128)(2,1)}), bf16[2,32,3584]{2,1,0:T(8,128)(2,1)S(1)}, u32[]{:S(2)}, u32[]{:S(2)}) async-start(bf16[2,32,3584]{2,1,0:T(8,128)(2,1)} %bitcast.16), calls=%async_computation.3 | async-start | bytes 917504 | tf_op jit(solution)/shard_map/all_to_all | solution.py:98
  188.0 0.0 copy-done
  188.1 0.7 fusion.23
  188.8 6.4 %all-to-all-done.3 = bf16[2,32,3584]{2,1,0:T(8,128)(2,1)S(1)} async-done(((bf16[2,32,3584]{2,1,0:T(8,128)(2,1)}), bf16[2,32,3584]{2,1,0:T(8,128)(2,1)S(1)}, u32[]{:S(2)}, u32[]{:S(2)}) %all-to-all-start.3) | async-done | bytes 458784 | tf_op jit(solution)/shard_map/all_to_all | solution.py:98
  195.2 0.8 reduce_sum.34
  (6 shorter events, 0.1 us)
Async XLA Ops:
  7.4 5.7 %copy-start.2 = (f32[128,2]{0,1:T(2,128)S(1)}, f32[128,2]{0,1:T(2,128)}, u32[]{:S(2)}) copy-start(f32[128,2]{0,1:T(2,128)} %param.11) | copy-start | bytes 3076
  20.0 72.2 %copy-start.1 = (bf16[1,384,1024]{2,1,0:T(8,128)(2,1)S(1)}, bf16[1,384,1024]{2,1,0:T(8,128)(2,1)}, u32[]{:S(2)}) copy-start(bf16[1,384,1024]{2,1,0:T(8,128)(2,1)} %param.13) | copy-start | bytes 2359300
  90.7 79.5 %collective-permute-start = (bf16[384,3584]{1,0:T(8,128)(2,1)S(1)}, bf16[384,3584]{1,0:T(8,128)(2,1)}, u32[]{:S(2)}, u32[]{:S(2)}) collective-permute-start(bf16[384,3584]{1,0:T(8,128)(2,1)S(1)} %bitcast.61), channel_id=1, source_target_pairs={{0,1},{1,0},{2,3},{3,2},{4,5},{5,4},{6,7},{7,6},{8,9},{9,8},{10,11... | collective-permute-start | bytes 8257544 | tf_op jit(solution)/shard_map/ppermute | solution.py:73
  93.3 67.7 %all-to-all-start = ((bf16[2,384,512]{1,2,0:T(8,128)(2,1)}), bf16[2,384,512]{1,2,0:T(8,128)(2,1)S(1)}, u32[]{:S(2)}, u32[]{:S(2)}) async-start(bf16[2,384,512]{1,2,0:T(8,128)(2,1)} %bitcast.3), calls=%async_computation | async-start | bytes 1572864 | tf_op jit(solution)/shard_map/all_to_all | solution.py:71
  161.0 9.1 %all-to-all-start.2 = ((bf16[2,32,512]{2,1,0:T(8,128)(2,1)}), bf16[2,32,512]{2,1,0:T(8,128)(2,1)}, u32[]{:S(2)}, u32[]{:S(2)}) async-start(bf16[2,32,512]{2,1,0:T(8,128)(2,1)} %copy.33), calls=%async_computation.2 | async-start | bytes 131072 | tf_op jit(solution)/shard_map/all_to_all | solution.py:91
  170.1 17.9 %copy-start = (bf16[128,384]{1,0:T(8,128)(2,1)S(1)}, bf16[128,384]{1,0:T(8,128)(2,1)}, u32[]{:S(2)}) copy-start(bf16[128,384]{1,0:T(8,128)(2,1)} %param.12) | copy-start | bytes 294916
  184.5 10.7 %all-to-all-start.3 = ((bf16[2,32,3584]{2,1,0:T(8,128)(2,1)}), bf16[2,32,3584]{2,1,0:T(8,128)(2,1)S(1)}, u32[]{:S(2)}, u32[]{:S(2)}) async-start(bf16[2,32,3584]{2,1,0:T(8,128)(2,1)} %bitcast.16), calls=%async_computation.3 | async-start | bytes 917504 | tf_op jit(solution)/shard_map/all_to_all | solution.py:98

commit v2 on v1

--- a/solution.py
+++ b/solution.py
@@ -1,6 +1,10 @@
+import functools
+
 import jax
 import jax.numpy as jnp
 from jax import lax
+from jax.experimental import pallas as pl
+from jax.experimental.pallas import tpu as pltpu
 from jax.sharding import PartitionSpec as P
 
 beta_one = 0.9
@@ -100,6 +104,362 @@
     return (refreshed.astype(jnp.bfloat16)[None], router_grad)
 
 
+MESH = pl.DeviceIdType.MESH
+
+
+def fused_kernel(
+    chunks,
+    grad_ref,
+    ids_ref,
+    combine_ref,
+    logits_ref,
+    hidden_hbm,
+    weight_hbm,
+    first_hbm,
+    second_hbm,
+    next_hbm,
+    refreshed_ref,
+    router_ref,
+    send,
+    rows,
+    hidden,
+    hidden_t,
+    weight,
+    first,
+    second,
+    following,
+    picks,
+    factors,
+    gradient,
+    updated,
+    product_own,
+    product_send,
+    product_recv,
+    send_sem,
+    recv_sem,
+    pass_send_sem,
+    pass_recv_sem,
+    local_sem,
+    own_sem,
+    side_send_sem,
+    side_recv_sem,
+    product_send_sem,
+    product_recv_sem,
+):
+    experts = send.shape[1]
+    capacity = send.shape[2]
+    width = send.shape[3]
+    slab = weight.shape[0]
+    tokens = grad_ref.shape[0]
+    count = experts * capacity
+    next_rows = following.shape[1]
+    groups = experts // 4
+    me = lax.axis_index("ep")
+    lane = lax.axis_index("dp")
+    other = 1 - lane
+    group, place = me // 4, me % 4
+
+    barrier = pltpu.get_barrier_semaphore()
+
+    @pl.loop(1, experts)
+    def _(step):
+        pl.semaphore_signal(
+            barrier, inc=1, device_id=((me + step) % experts, lane), device_id_type=MESH
+        )
+
+    pl.semaphore_signal(barrier, inc=1, device_id=(me, other), device_id_type=MESH)
+
+    own_columns = pl.ds(pl.multiple_of(lane * slab, slab), slab)
+    other_columns = pl.ds(pl.multiple_of(other * slab, slab), slab)
+    loads = [
+        pltpu.make_async_copy(hidden_hbm.at[:, own_columns], hidden.at[0], local_sem.at[0]),
+        pltpu.make_async_copy(next_hbm.at[:, own_columns], following.at[0], local_sem.at[1]),
+        pltpu.make_async_copy(weight_hbm, weight, local_sem.at[2]),
+        pltpu.make_async_copy(first_hbm, first, local_sem.at[3]),
+        pltpu.make_async_copy(second_hbm, second, local_sem.at[4]),
+    ]
+    for load in loads:
+        load.start()
+
+    ids = ids_ref[...]
+    weights = combine_ref[...]
+    expert_of = lax.broadcasted_iota(jnp.int32, (experts, tokens), 0)
+    named = [(ids[k : k + 1, :] == expert_of) for k in range(ids.shape[0])]
+    chosen = sum(jnp.where(hit, 1.0, 0.0) for hit in named)
+    factor_of = sum(jnp.where(hit, weights[k : k + 1, :], 0.0) for k, hit in enumerate(named))
+    earlier = lax.broadcasted_iota(jnp.int32, (tokens, tokens), 0) < lax.broadcasted_iota(
+        jnp.int32, (tokens, tokens), 1
+    )
+    before = jnp.dot(
+        chosen.astype(jnp.bfloat16),
+        jnp.where(earlier, 1.0, 0.0).astype(jnp.bfloat16),
+        preferred_element_type=jnp.float32,
+    )
+    before = jnp.where(chosen > 0.5, before, -1.0)
+    slot = lax.broadcasted_iota(jnp.int32, (capacity, tokens), 0).astype(jnp.float32)
+    for e in range(experts):
+        pick = jnp.where(before[e : e + 1, :] == slot, 1.0, 0.0)
+        picks[e * capacity : (e + 1) * capacity, :] = pick
+        factors[e * capacity : (e + 1) * capacity, :] = jnp.broadcast_to(
+            jnp.sum(pick * factor_of[e : e + 1, :], axis=1, keepdims=True), (capacity, 128)
+        )
+
+    def peer(step):
+        return ((group + step // 4) % groups) * 4 + (place + step) % 4
+
+    def source(step):
+        return ((group + groups - step // 4) % groups) * 4 + (place + 4 - step % 4) % 4
+
+    def order(step):
+        return (step + experts // 2) % experts
+
+    def routed(c, step):
+        to = peer(step)
+        return pltpu.make_async_remote_copy(
+            src_ref=send.at[c, to],
+            dst_ref=rows.at[c, me],
+            send_sem=send_sem.at[c, step],
+            recv_sem=recv_sem.at[c, step],
+            device_id=(to, lane),
+            device_id_type=MESH,
+        )
+
+    def passed(c, step, src):
+        return pltpu.make_async_remote_copy(
+            src_ref=src,
+            dst_ref=rows.at[c, experts + source(step)],
+            send_sem=pass_send_sem.at[c, step],
+            recv_sem=pass_recv_sem.at[c, step],
+            device_id=(me, other),
+            device_id_type=MESH,
+        )
+
+    sides = [
+        pltpu.make_async_remote_copy(
+            src_ref=src.at[:, other_columns],
+            dst_ref=dst.at[1],
+            send_sem=side_send_sem.at[i],
+            recv_sem=side_recv_sem.at[i],
+            device_id=(me, other),
+            device_id_type=MESH,
+        )
+        for i, (src, dst) in enumerate(((hidden_hbm, hidden), (next_hbm, following)))
+    ]
+
+    chosen_rows = picks[...].astype(jnp.bfloat16)
+    factor = factors[:, 0:1]
+
+    def own_copy(c):
+        return pltpu.make_async_copy(send.at[c, me], rows.at[c, me], own_sem.at[c])
+
+    for c in range(chunks):
+        picked = jnp.dot(
+            chosen_rows,
+            grad_ref[:, c * width : (c + 1) * width],
+            preferred_element_type=jnp.float32,
+        )
+        send[c] = (picked * factor).reshape(experts, capacity, width).astype(jnp.bfloat16)
+        if c == 0:
+            pl.semaphore_wait(barrier, experts)
+
+        @pl.loop(0, experts)
+        def _(index):
+            step = order(index)
+
+            @pl.when(step != 0)
+            def _():
+                routed(c, step).start()
+
+        passed(c, 0, send.at[c, me]).start()
+        own_copy(c).start()
+        if c == 0:
+            for side in sides:
+                side.start()
+
+    logits = logits_ref[...].astype(jnp.float32)
+    row_max = jnp.max(logits, axis=-1, keepdims=True)
+    log_total = row_max + jnp.log(jnp.sum(jnp.exp(logits - row_max), axis=-1, keepdims=True))
+    router_ref[...] = (zloss_coef * 2.0 * log_total * jnp.exp(logits - log_total)).astype(
+        jnp.bfloat16
+    )
+    for load in loads:
+        load.wait()
+    hidden_t[:, 0:count] = hidden[0].astype(jnp.float32).T.astype(jnp.bfloat16)
+
+    def collect(c):
+        @pl.loop(0, experts)
+        def _(index):
+            step = order(index)
+
+            @pl.when(step != 0)
+            def _():
+                routed(c, step).wait_recv()
+                passed(c, step, rows.at[c, source(step)]).start()
+
+        own_copy(c).wait()
+
+    def finish(c):
+        @pl.loop(0, experts)
+        def _(step):
+            passed(c, step, rows.at[c, source(step)]).wait_recv()
+
+        columns = slice(c * width, (c + 1) * width)
+        gradient[...] = jnp.dot(
+            hidden_t[...],
+            rows[c].reshape(2 * count, width),
+            preferred_element_type=jnp.float32,
+        )
+
+        @pl.loop(0, slab // 16)
+        def _(block):
+            part = pl.ds(pl.multiple_of(block * 16, 16), 16)
+            slope = gradient[part, :]
+            first_new = beta_one * first[part, columns].astype(jnp.float32) + (
+                1.0 - beta_one
+            ) * slope
+            second_new = beta_two * second[part, columns].astype(jnp.float32) + (
+                1.0 - beta_two
+            ) * slope * slope
+            first_hat = first_new * (1.0 / (1.0 - beta_one**step_count))
+            second_hat = second_new * (1.0 / (1.0 - beta_two**step_count))
+            current = weight[part, columns].astype(jnp.float32)
+            change = first_hat / (jnp.sqrt(second_hat) + adam_eps) + decay_rate * current
+            updated[part, :] = (current - learn_rate * change).astype(jnp.bfloat16)
+
+        product = jnp.dot(
+            following[...].reshape(2 * next_rows, slab),
+            updated[...],
+            preferred_element_type=jnp.float32,
+        )
+        product_own[c] = product[:next_rows]
+        product_send[c] = product[next_rows:].astype(jnp.bfloat16)
+        shared(c).start()
+
+    def shared(c):
+        return pltpu.make_async_remote_copy(
+            src_ref=product_send.at[c],
+            dst_ref=product_recv.at[c],
+            send_sem=product_send_sem.at[c],
+            recv_sem=product_recv_sem.at[c],
+            device_id=(me, other),
+            device_id_type=MESH,
+        )
+
+    collect(0)
+    for side in sides:
+        side.wait()
+    hidden_t[:, count : 2 * count] = hidden[1].astype(jnp.float32).T.astype(jnp.bfloat16)
+    for c in range(chunks):
+        if c + 1 < chunks:
+            collect(c + 1)
+        finish(c)
+
+    for c in range(chunks):
+        shared(c).wait()
+        refreshed_ref[:, c * width : (c + 1) * width] = (
+            product_own[c] + product_recv[c].astype(jnp.float32)
+        ).astype(jnp.bfloat16)
+
+        @pl.loop(0, experts)
+        def _(step):
+            @pl.when(step != 0)
+            def _():
+                routed(c, step).wait_send()
+
+            passed(c, step, rows.at[c, source(step)]).wait_send()
+
+
+def fused(
+    out_grad,
+    expert_ids,
+    combine,
+    router_logits,
+    saved_hidden,
+    weight,
+    moment_one,
+    moment_two,
+    next_hidden,
+):
+    experts = lax.axis_size("ep")
+    count, _ = saved_hidden.shape[1:]
+    capacity = count // experts
+    tokens, model_width = out_grad.shape
+    slab = weight.shape[1]
+    next_rows = next_hidden.shape[1]
+    chunks = 4
+    width = model_width // chunks
+    vmem = pl.BlockSpec(memory_space=pltpu.VMEM)
+    hbm = pl.BlockSpec(memory_space=pl.ANY)
+    dma = pltpu.SemaphoreType.DMA
+    flops = 2 * slab * 2 * count * model_width + 4 * next_rows * slab * model_width
+    refreshed, router_grad = pl.pallas_call(
+        functools.partial(fused_kernel, chunks),
+        out_shape=(
+            jax.ShapeDtypeStruct((next_rows, model_width), jnp.bfloat16),
+            jax.ShapeDtypeStruct(router_logits.shape, jnp.bfloat16),
+        ),
+        in_specs=[vmem] * 4 + [hbm] * 5,
+        out_specs=(vmem, vmem),
+        scratch_shapes=[
+            pltpu.VMEM((chunks, experts, capacity, width), jnp.bfloat16),
+            pltpu.VMEM((chunks, 2 * experts, capacity, width), jnp.bfloat16),
+            pltpu.VMEM((2, count, slab), jnp.bfloat16),
+            pltpu.VMEM((slab, 2 * count), jnp.bfloat16),
+            pltpu.VMEM((slab, model_width), jnp.bfloat16),
+            pltpu.VMEM((slab, model_width), jnp.bfloat16),
+            pltpu.VMEM((slab, model_width), jnp.bfloat16),
+            pltpu.VMEM((2, next_rows, slab), jnp.bfloat16),
+            pltpu.VMEM((count, tokens), jnp.float32),
+            pltpu.VMEM((count, 128), jnp.float32),
+            pltpu.VMEM((slab, width), jnp.float32),
+            pltpu.VMEM((slab, width), jnp.bfloat16),
+            pltpu.VMEM((chunks, next_rows, width), jnp.float32),
+            pltpu.VMEM((chunks, next_rows, width), jnp.bfloat16),
+            pltpu.VMEM((chunks, next_rows, width), jnp.bfloat16),
+            dma((chunks, experts)),
+            dma((chunks, experts)),
+            dma((chunks, experts)),
+            dma((chunks, experts)),
+            dma((5,)),
+            dma((chunks,)),
+            dma((2,)),
+            dma((2,)),
+            dma((chunks,)),
+            dma((chunks,)),
+        ],
+        compiler_params=pltpu.CompilerParams(
+            collective_id=0, has_side_effects=True, vmem_limit_bytes=58 * 2**20
+        ),
+        cost_estimate=pl.CostEstimate(
+            flops=flops, bytes_accessed=8 * slab * model_width, transcendentals=0
+        ),
+        name="fused_expert_step",
+    )(
+        out_grad,
+        expert_ids.T,
+        combine.T,
+        router_logits,
+        saved_hidden[0],
+        weight[0],
+        moment_one[0],
+        moment_two[0],
+        next_hidden[0],
+    )
+    return refreshed[None], router_grad
+
+
+def fits(mesh, saved_hidden, weight, out_grad):
+    experts, replicas = mesh.shape["ep"], mesh.shape["dp"]
+    capacity = saved_hidden.shape[1] // (experts * replicas)
+    return (
+        replicas == 2
+        and experts % 4 == 0
+        and capacity % 8 == 0
+        and (weight.shape[1] // replicas) % 128 == 0
+        and out_grad.shape[1] % 512 == 0
+    )
+
+
 def solution(mesh):
     in_specs = (
         P(("ep", "dp"), None),
@@ -113,6 +473,11 @@
         P("ep", "dp", None),
     )
     out_specs = (P("ep", "dp", None), P(("ep", "dp"), None))
-    return jax.shard_map(
-        per_device, mesh=mesh, in_specs=in_specs, out_specs=out_specs, check_vma=False
-    )
+
+    def run(*arrays):
+        body = fused if fits(mesh, arrays[4], arrays[5], arrays[0]) else per_device
+        return jax.shard_map(
+            body, mesh=mesh, in_specs=in_specs, out_specs=out_specs, check_vma=False
+        )(*arrays)
+
+    return run

time: 197 us -> 102 us (0.52)
  the two profiles are of different devices: /device:TPU:0 before, /device:TPU:9 now
where the time goes in v2:
time: 102 us; the launch traced here: 101 us
  Pallas kernels  97.5 us (96%)
  local copies, waits for them, and re-layouts  3.18 us (3%)
    pallas_call x1, Pallas kernels, fused(): pl.pallas_call(functools.partial(fused_kernel, chunks), out_shape=(jax.Sh...  97.5 us
    unnamed x2, local copies, waits for them, and re-layouts  3.18 us

profile of v2, /device:TPU:9, one launch (start us, length us, event | category | flops | bytes accessed | tf_op | source)
XLA Modules:
  0.0 101.3 jit_solution(6359430785338774141)
XLA Ops:
  0.6 97.5 %fused_expert_step.1 = (bf16[32,3584]{1,0:T(8,128)(2,1)}, bf16[128,384]{1,0:T(8,128)(2,1)}) custom-call(bf16[128,3584]{1,0:T(8,128)(2,1)} %grad_ref.1, s32[2,128]{1,0:T(2,128)} %bitcast.14, f32[2,128]{1,0:T(2,128)} %bitcast.15, bf16[128,384]{1,0:T(8,128)(2,1)} %logits_ref.1, bf16[384,1024]{1,0:T(8,128)(2,1)} %bitcast.11, bf16[512,3584]{1,0:T(8,128)(2,1)} %bitcast.8, ...), custom_call_target="tpu_custom_call" | custom-call | flops 3053453312 | bytes 14680064 | tf_op jit(solution)/shard_map/fused_expert_step/pallas_call | solution.py:395
  98.2 1.6 %copy.13 = bf16[1,32,3584]{2,1,0:T(8,128)(2,1)} copy(bf16[1,32,3584]{2,1,0:T(8,128)(2,1)} %bitcast.12) | data formatting | bytes 458752
  99.8 1.5 %copy.14 = bf16[128,384]{1,0:T(8,128)(2,1)} copy(bf16[128,384]{1,0:T(8,128)(2,1)} %get-tuple-element.9) | data formatting | bytes 196608

commit v3 on v2

--- a/solution.py
+++ b/solution.py
@@ -110,8 +110,7 @@
 def fused_kernel(
     chunks,
     grad_ref,
-    ids_ref,
-    combine_ref,
+    table_ref,
     logits_ref,
     hidden_hbm,
     weight_hbm,
@@ -130,6 +129,11 @@
     following,
     picks,
     factors,
+    peer_picks,
+    peer_factors,
+    peer_table,
+    peer_grad,
+    near_send,
     gradient,
     updated,
     product_own,
@@ -145,6 +149,12 @@
     side_recv_sem,
     product_send_sem,
     product_recv_sem,
+    near_send_sem,
+    near_recv_sem,
+    near_own_sem,
+    raw_send_sem,
+    raw_recv_sem,
+    table_sem,
 ):
     experts = send.shape[1]
     capacity = send.shape[2]
@@ -153,11 +163,13 @@
     tokens = grad_ref.shape[0]
     count = experts * capacity
     next_rows = following.shape[1]
-    groups = experts // 4
+    half = experts // 2
     me = lax.axis_index("ep")
     lane = lax.axis_index("dp")
     other = 1 - lane
-    group, place = me // 4, me % 4
+    side, place = me // half, me % half
+    near_base = side * half
+    far_base = (1 - side) * half
 
     barrier = pltpu.get_barrier_semaphore()
 
@@ -181,40 +193,14 @@
     for load in loads:
         load.start()
 
-    ids = ids_ref[...]
-    weights = combine_ref[...]
-    expert_of = lax.broadcasted_iota(jnp.int32, (experts, tokens), 0)
-    named = [(ids[k : k + 1, :] == expert_of) for k in range(ids.shape[0])]
-    chosen = sum(jnp.where(hit, 1.0, 0.0) for hit in named)
-    factor_of = sum(jnp.where(hit, weights[k : k + 1, :], 0.0) for k, hit in enumerate(named))
-    earlier = lax.broadcasted_iota(jnp.int32, (tokens, tokens), 0) < lax.broadcasted_iota(
-        jnp.int32, (tokens, tokens), 1
-    )
-    before = jnp.dot(
-        chosen.astype(jnp.bfloat16),
-        jnp.where(earlier, 1.0, 0.0).astype(jnp.bfloat16),
-        preferred_element_type=jnp.float32,
-    )
-    before = jnp.where(chosen > 0.5, before, -1.0)
-    slot = lax.broadcasted_iota(jnp.int32, (capacity, tokens), 0).astype(jnp.float32)
-    for e in range(experts):
-        pick = jnp.where(before[e : e + 1, :] == slot, 1.0, 0.0)
-        picks[e * capacity : (e + 1) * capacity, :] = pick
-        factors[e * capacity : (e + 1) * capacity, :] = jnp.broadcast_to(
-            jnp.sum(pick * factor_of[e : e + 1, :], axis=1, keepdims=True), (capacity, 128)
-        )
-
-    def peer(step):
-        return ((group + step // 4) % groups) * 4 + (place + step) % 4
-
-    def source(step):
-        return ((group + groups - step // 4) % groups) * 4 + (place + 4 - step % 4) % 4
-
-    def order(step):
-        return (step + experts // 2) % experts
-
-    def routed(c, step):
-        to = peer(step)
+    def shift(step):
+        return (place + step) % half
+
+    def shift_back(step):
+        return (place + half - step) % half
+
+    def routed(c, step, base):
+        to = base + shift(step)
         return pltpu.make_async_remote_copy(
             src_ref=send.at[c, to],
             dst_ref=rows.at[c, me],
@@ -224,84 +210,146 @@
             device_id_type=MESH,
         )
 
-    def passed(c, step, src):
+    def near(c, step):
         return pltpu.make_async_remote_copy(
-            src_ref=src,
-            dst_ref=rows.at[c, experts + source(step)],
+            src_ref=near_send.at[c, shift(step)],
+            dst_ref=rows.at[c, experts + me],
+            send_sem=near_send_sem.at[c, step],
+            recv_sem=near_recv_sem.at[c, step],
+            device_id=(near_base + shift(step), lane),
+            device_id_type=MESH,
+        )
+
+    def passed(c, step):
+        origin = far_base + shift_back(step)
+        return pltpu.make_async_remote_copy(
+            src_ref=rows.at[c, origin],
+            dst_ref=rows.at[c, experts + origin],
             send_sem=pass_send_sem.at[c, step],
             recv_sem=pass_recv_sem.at[c, step],
             device_id=(me, other),
             device_id_type=MESH,
         )
 
-    sides = [
-        pltpu.make_async_remote_copy(
-            src_ref=src.at[:, other_columns],
-            dst_ref=dst.at[1],
-            send_sem=side_send_sem.at[i],
-            recv_sem=side_recv_sem.at[i],
+    def to_other(src, dst, send_one, recv_one):
+        return pltpu.make_async_remote_copy(
+            src_ref=src,
+            dst_ref=dst,
+            send_sem=send_one,
+            recv_sem=recv_one,
             device_id=(me, other),
             device_id_type=MESH,
         )
+
+    def raw(c):
+        return to_other(
+            grad_ref.at[:, c * width : (c + 1) * width],
+            peer_grad.at[c],
+            raw_send_sem.at[c],
+            raw_recv_sem.at[c],
+        )
+
+    table_copy = to_other(table_ref, peer_table, table_sem.at[0], table_sem.at[1])
+    sides = [
+        to_other(src.at[:, other_columns], dst.at[1], side_send_sem.at[i], side_recv_sem.at[i])
         for i, (src, dst) in enumerate(((hidden_hbm, hidden), (next_hbm, following)))
     ]
 
-    chosen_rows = picks[...].astype(jnp.bfloat16)
-    factor = factors[:, 0:1]
-
     def own_copy(c):
         return pltpu.make_async_copy(send.at[c, me], rows.at[c, me], own_sem.at[c])
 
-    for c in range(chunks):
+    def near_own_copy(c):
+        return pltpu.make_async_copy(
+            near_send.at[c, place], rows.at[c, experts + me], near_own_sem.at[c]
+        )
+
+    def make_picks(table, base, wanted, picks_out, factors_out):
+        top = table.shape[0] // 2
+        expert_of = lax.broadcasted_iota(jnp.int32, (wanted, tokens), 0) + base
+        expert_of = expert_of.astype(jnp.float32)
+        named = [(table[k : k + 1, :] == expert_of) for k in range(top)]
+        chosen = sum(jnp.where(hit, 1.0, 0.0) for hit in named)
+        factor_of = sum(
+            jnp.where(hit, table[top + k : top + k + 1, :], 0.0) for k, hit in enumerate(named)
+        )
+        earlier = lax.broadcasted_iota(jnp.int32, (tokens, tokens), 0) < lax.broadcasted_iota(
+            jnp.int32, (tokens, tokens), 1
+        )
+        before = jnp.dot(
+            chosen.astype(jnp.bfloat16),
+            jnp.where(earlier, 1.0, 0.0).astype(jnp.bfloat16),
+            preferred_element_type=jnp.float32,
+        )
+        before = jnp.where(chosen > 0.5, before, -1.0)
+        slot = lax.broadcasted_iota(jnp.int32, (capacity, tokens), 0).astype(jnp.float32)
+        for e in range(wanted):
+            pick = jnp.where(before[e : e + 1, :] == slot, 1.0, 0.0)
+            picks_out[e * capacity : (e + 1) * capacity, :] = pick
+            factors_out[e * capacity : (e + 1) * capacity, :] = jnp.broadcast_to(
+                jnp.sum(pick * factor_of[e : e + 1, :], axis=1, keepdims=True), (capacity, 128)
+            )
+
+    def send_own(c):
         picked = jnp.dot(
-            chosen_rows,
+            picks[...].astype(jnp.bfloat16),
             grad_ref[:, c * width : (c + 1) * width],
             preferred_element_type=jnp.float32,
         )
-        send[c] = (picked * factor).reshape(experts, capacity, width).astype(jnp.bfloat16)
-        if c == 0:
-            pl.semaphore_wait(barrier, experts)
-
-        @pl.loop(0, experts)
-        def _(index):
-            step = order(index)
-
-            @pl.when(step != 0)
-            def _():
-                routed(c, step).start()
-
-        passed(c, 0, send.at[c, me]).start()
+        scaled = picked * factors[:, 0:1]
+        send[c] = scaled.reshape(experts, capacity, width).astype(jnp.bfloat16)
+
+        @pl.loop(0, half)
+        def _(step):
+            routed(c, half + step, far_base).start()
+
+        @pl.loop(1, half)
+        def _(step):
+            routed(c, step, near_base).start()
+
         own_copy(c).start()
-        if c == 0:
-            for side in sides:
-                side.start()
-
-    logits = logits_ref[...].astype(jnp.float32)
-    row_max = jnp.max(logits, axis=-1, keepdims=True)
-    log_total = row_max + jnp.log(jnp.sum(jnp.exp(logits - row_max), axis=-1, keepdims=True))
-    router_ref[...] = (zloss_coef * 2.0 * log_total * jnp.exp(logits - log_total)).astype(
-        jnp.bfloat16
-    )
-    for load in loads:
-        load.wait()
-    hidden_t[:, 0:count] = hidden[0].astype(jnp.float32).T.astype(jnp.bfloat16)
+
+    def send_near(c):
+        raw(c).wait_recv()
+        picked = jnp.dot(
+            peer_picks[...].astype(jnp.bfloat16),
+            peer_grad[c],
+            preferred_element_type=jnp.float32,
+        )
+        scaled = picked * peer_factors[:, 0:1]
+        near_send[c] = scaled.reshape(half, capacity, width).astype(jnp.bfloat16)
+
+        @pl.loop(1, half)
+        def _(step):
+            near(c, step).start()
+
+        near_own_copy(c).start()
+
+    def router_part():
+        logits = logits_ref[...].astype(jnp.float32)
+        row_max = jnp.max(logits, axis=-1, keepdims=True)
+        log_total = row_max + jnp.log(jnp.sum(jnp.exp(logits - row_max), axis=-1, keepdims=True))
+        router_ref[...] = (zloss_coef * 2.0 * log_total * jnp.exp(logits - log_total)).astype(
+            jnp.bfloat16
+        )
 
     def collect(c):
-        @pl.loop(0, experts)
-        def _(index):
-            step = order(index)
-
-            @pl.when(step != 0)
-            def _():
-                routed(c, step).wait_recv()
-                passed(c, step, rows.at[c, source(step)]).start()
+        @pl.loop(0, half)
+        def _(step):
+            routed(c, half + step, far_base).wait_recv()
+            passed(c, step).start()
+
+    def finish(c):
+        @pl.loop(1, half)
+        def _(step):
+            routed(c, step, near_base).wait_recv()
+            near(c, step).wait_recv()
 
         own_copy(c).wait()
-
-    def finish(c):
-        @pl.loop(0, experts)
-        def _(step):
-            passed(c, step, rows.at[c, source(step)]).wait_recv()
+        near_own_copy(c).wait()
+
+        @pl.loop(0, half)
+        def _(step):
+            passed(c, step).wait_recv()
 
         columns = slice(c * width, (c + 1) * width)
         gradient[...] = jnp.dot(
@@ -336,37 +384,61 @@
         shared(c).start()
 
     def shared(c):
-        return pltpu.make_async_remote_copy(
-            src_ref=product_send.at[c],
-            dst_ref=product_recv.at[c],
-            send_sem=product_send_sem.at[c],
-            recv_sem=product_recv_sem.at[c],
-            device_id=(me, other),
-            device_id_type=MESH,
-        )
-
+        return to_other(
+            product_send.at[c], product_recv.at[c], product_send_sem.at[c], product_recv_sem.at[c]
+        )
+
+    pl.semaphore_wait(barrier, experts)
+    table_copy.start()
+    raw(0).start()
+    raw(1).start()
+    make_picks(table_ref[...], 0, experts, picks, factors)
+    send_own(0)
+    table_copy.wait_recv()
+    make_picks(peer_table[...], near_base, half, peer_picks, peer_factors)
+    send_near(0)
+    raw(2).start()
+    send_own(1)
+    router_part()
+    send_near(1)
+    for c in range(3, chunks):
+        raw(c).start()
+    for one in sides:
+        one.start()
+    send_own(2)
+    for load in loads:
+        load.wait()
+    hidden_t[:, 0:count] = hidden[0].astype(jnp.float32).T.astype(jnp.bfloat16)
     collect(0)
-    for side in sides:
-        side.wait()
+    send_near(2)
+    for c in range(3, chunks):
+        send_own(c)
+        send_near(c)
+    for one in sides:
+        one.wait()
     hidden_t[:, count : 2 * count] = hidden[1].astype(jnp.float32).T.astype(jnp.bfloat16)
     for c in range(chunks):
         if c + 1 < chunks:
             collect(c + 1)
         finish(c)
 
+    table_copy.wait_send()
     for c in range(chunks):
         shared(c).wait()
         refreshed_ref[:, c * width : (c + 1) * width] = (
             product_own[c] + product_recv[c].astype(jnp.float32)
         ).astype(jnp.bfloat16)
-
-        @pl.loop(0, experts)
-        def _(step):
-            @pl.when(step != 0)
-            def _():
-                routed(c, step).wait_send()
-
-            passed(c, step, rows.at[c, source(step)]).wait_send()
+        raw(c).wait_send()
+
+        @pl.loop(0, half)
+        def _(step):
+            routed(c, half + step, far_base).wait_send()
+            passed(c, step).wait_send()
+
+        @pl.loop(1, half)
+        def _(step):
+            routed(c, step, near_base).wait_send()
+            near(c, step).wait_send()
 
 
 def fused(
@@ -388,6 +460,7 @@
     next_rows = next_hidden.shape[1]
     chunks = 4
     width = model_width // chunks
+    table = jnp.concatenate([expert_ids.T.astype(jnp.float32), combine.T])
     vmem = pl.BlockSpec(memory_space=pltpu.VMEM)
     hbm = pl.BlockSpec(memory_space=pl.ANY)
     dma = pltpu.SemaphoreType.DMA
@@ -398,7 +471,7 @@
             jax.ShapeDtypeStruct((next_rows, model_width), jnp.bfloat16),
             jax.ShapeDtypeStruct(router_logits.shape, jnp.bfloat16),
         ),
-        in_specs=[vmem] * 4 + [hbm] * 5,
+        in_specs=[vmem] * 3 + [hbm] * 5,
         out_specs=(vmem, vmem),
         scratch_shapes=[
             pltpu.VMEM((chunks, experts, capacity, width), jnp.bfloat16),
@@ -411,6 +484,11 @@
             pltpu.VMEM((2, next_rows, slab), jnp.bfloat16),
             pltpu.VMEM((count, tokens), jnp.float32),
             pltpu.VMEM((count, 128), jnp.float32),
+            pltpu.VMEM((count // 2, tokens), jnp.float32),
+            pltpu.VMEM((count // 2, 128), jnp.float32),
+            pltpu.VMEM(table.shape, jnp.float32),
+            pltpu.VMEM((chunks, tokens, width), jnp.bfloat16),
+            pltpu.VMEM((chunks, experts // 2, capacity, width), jnp.bfloat16),
             pltpu.VMEM((slab, width), jnp.float32),
             pltpu.VMEM((slab, width), jnp.bfloat16),
             pltpu.VMEM((chunks, next_rows, width), jnp.float32),
@@ -418,14 +496,20 @@
             pltpu.VMEM((chunks, next_rows, width), jnp.bfloat16),
             dma((chunks, experts)),
             dma((chunks, experts)),
-            dma((chunks, experts)),
-            dma((chunks, experts)),
+            dma((chunks, experts // 2)),
+            dma((chunks, experts // 2)),
             dma((5,)),
             dma((chunks,)),
             dma((2,)),
             dma((2,)),
             dma((chunks,)),
             dma((chunks,)),
+            dma((chunks, experts // 2)),
+            dma((chunks, experts // 2)),
+            dma((chunks,)),
+            dma((chunks,)),
+            dma((chunks,)),
+            dma((2,)),
         ],
         compiler_params=pltpu.CompilerParams(
             collective_id=0, has_side_effects=True, vmem_limit_bytes=58 * 2**20
@@ -436,8 +520,7 @@
         name="fused_expert_step",
     )(
         out_grad,
-        expert_ids.T,
-        combine.T,
+        table,
         router_logits,
         saved_hidden[0],
         weight[0],

time: 102 us -> 88.6 us (0.87)
  the two profiles are of different devices: /device:TPU:9 before, /device:TPU:0 now
where the time goes in v3:
time: 88.6 us; the launch traced here: 88.3 us
  Pallas kernels  82.6 us (93%)
  local copies, waits for them, and re-layouts  3.18 us (4%)
  other arithmetic  1.94 us (2%)
    pallas_call x1, Pallas kernels, fused(): pl.pallas_call(functools.partial(fused_kernel, chunks), out_shape=(jax.Sh...  82.6 us
    unnamed x2, local copies, waits for them, and re-layouts  3.18 us

profile of v3, /device:TPU:0, one launch (start us, length us, event | category | flops | bytes accessed | tf_op | source)
XLA Modules:
  0.0 88.3 jit_solution(3286720089279280280)
XLA Ops:
  0.6 0.7 convert_bitcast_fusion
  1.3 1.3 %pad_maximum_fusion.table_ref = f32[4,128]{1,0:T(4,128)} fusion(f32[2,128]{1,0:T(2,128)} %bitcast.15, f32[2,128]{1,0:T(2,128)S(1)} %convert_bitcast_fusion), kind=kLoop, calls=%fused_computation | loop fusion | flops 512 | bytes 4096 | tf_op jit(solution)/shard_map/concatenate | solution.py:463
  2.6 82.6 %fused_expert_step.1 = (bf16[32,3584]{1,0:T(8,128)(2,1)}, bf16[128,384]{1,0:T(8,128)(2,1)}) custom-call(bf16[128,3584]{1,0:T(8,128)(2,1)} %grad_ref.1, f32[4,128]{1,0:T(4,128)} %pad_maximum_fusion.table_ref, bf16[128,384]{1,0:T(8,128)(2,1)} %logits_ref.1, bf16[384,1024]{1,0:T(8,128)(2,1)} %bitcast.12, bf16[512,3584]{1,0:T(8,128)(2,1)} %bitcast.9, ...), custom_call_target="tpu_custom_call" | custom-call | flops 3053453312 | bytes 14680064 | tf_op jit(solution)/shard_map/fused_expert_step/pallas_call | solution.py:468
  85.1 1.6 %copy.13 = bf16[1,32,3584]{2,1,0:T(8,128)(2,1)} copy(bf16[1,32,3584]{2,1,0:T(8,128)(2,1)} %bitcast.13) | data formatting | bytes 458752
  86.8 1.5 %copy.14 = bf16[128,384]{1,0:T(8,128)(2,1)} copy(bf16[128,384]{1,0:T(8,128)(2,1)} %get-tuple-element.9) | data formatting | bytes 196608
